TPU v7x, 512 devices: a whole 4x4x16 slice. The times are simulated.
512 devices in a mesh: row: 16 (over y, x), col: 16 (over z), dep: 2 (over core).
Axes of the slice: x: 4, y: 4, z: 16, core: 2. Of those that a mesh axis runs over, the one named last changes fastest.
Arguments:
- features: bfloat16 [32768, 256], P(('col', 'row')), may hold values from -6 to 6
- weight: bfloat16 [256, 256], P(None, 'dep'), may hold values from -0.375 to 0.375
- tiles: bfloat16 [16, 16, 128, 128, 128], P('row', 'col'), may hold values from -0.1875 to 0.1875
- tile_blocks: int32 [16, 16, 2, 128], P('row', 'col'), may hold values from 0 to 15, as said below
- tile_counts: int32 [16, 16], P('row', 'col'), may hold values from 16 to 128, as said below
- cotangent: bfloat16 [32768, 256], P(('row', 'col'), 'dep'), may hold values from -6 to 6
Outputs:
- activations: bfloat16 [32768, 256], P(('row', 'col'), 'dep')
- feature_grad: bfloat16 [32768, 256], P(('col', 'row'), 'dep')
- weight_grad: float32 [256, 256], P(None, 'dep')
Inputs may be any that keep to these rules, and one draw needn't show every extreme that they name: `tile_blocks`: live slots of one grid position name distinct block pairs; padding slots also hold valid block numbers. `tile_counts`: each count is 128 divided by 1, 2, 4 or 8; at least one grid position holds exactly 128 live slots.
All inputs are finite; a program needn't handle non-finite values.
Results may differ from a plain program's by a relative error of at most 0.034.
Values may be sent and summed in bfloat16 or wider, within the bound.
A program may use at most 64 MiB of HBM per device.

v0:
```python
import jax
import jax.numpy as jnp
from jax import lax
from jax.sharding import PartitionSpec as P

BLOCK = 128
BPP = 16


def chosen_column_sum(select_half, product, form):
    upper = product.astype(jnp.bfloat16)
    lower = (product - upper.astype(jnp.float32)).astype(jnp.bfloat16)
    first = jnp.einsum(form, select_half, upper, preferred_element_type=jnp.float32)
    second = jnp.einsum(form, select_half, lower, preferred_element_type=jnp.float32)
    return first + second


def per_device(features, weight, tiles, tile_blocks, tile_counts, cotangent):
    tile_set = tiles[0, 0]
    slot_total = tile_set.shape[0]
    block_rows = tile_blocks[0, 0, 0]
    block_column_count = tile_blocks[0, 0, 1]
    live = jnp.arange(slot_total, dtype=jnp.int32) < tile_counts[0, 0]
    panel_slots = jnp.arange(BPP, dtype=jnp.int32)
    row_select = ((block_rows[None, :] == panel_slots[:, None]) & live[None, :]).astype(
        jnp.bfloat16
    )
    column_choice_mask = (
        (block_column_count[None, :] == panel_slots[:, None]) & live[None, :]
    ).astype(jnp.bfloat16)
    half_width = weight.shape[1]
    projected = jnp.dot(features, weight, preferred_element_type=jnp.float32).astype(jnp.bfloat16)
    source_all = lax.all_gather(projected, "row", axis=0, tiled=True)
    source_tiles = source_all.reshape(BPP, BLOCK, half_width)[block_column_count]
    product = jnp.einsum("tab,tbf->taf", tile_set, source_tiles, preferred_element_type=jnp.float32)
    partial_value = chosen_column_sum(row_select, product, "rt,taf->raf")
    partial_value = partial_value.reshape(BPP * BLOCK, half_width)
    share = lax.psum_scatter(partial_value, "col", scatter_dimension=0, tiled=True)
    squash = jnp.tanh(share)
    activations = squash.astype(jnp.bfloat16)
    slope = (cotangent.astype(jnp.float32) * (1.0 - squash * squash)).astype(jnp.bfloat16)
    slope_all = lax.all_gather(slope, "col", axis=0, tiled=True)
    slope_tiles = slope_all.reshape(BPP, BLOCK, half_width)[block_rows]
    backward_product_terms = jnp.einsum(
        "tab,taf->tbf", tile_set, slope_tiles, preferred_element_type=jnp.float32
    )
    backward_partial_sum = chosen_column_sum(
        column_choice_mask, backward_product_terms, "pl,leh->peh"
    )
    backward_partial_sum = backward_partial_sum.reshape(BPP * BLOCK, half_width)
    spread = lax.psum_scatter(
        backward_partial_sum.astype(jnp.bfloat16), "row", scatter_dimension=0, tiled=True
    )
    weight_product_terms = lax.dot_general(
        features, spread, (((0,), (0,)), ((), ())), preferred_element_type=jnp.float32
    )
    weight_grad = lax.psum(weight_product_terms, ("row", "col"))
    terms = lax.dot_general(
        spread, weight, (((1,), (1,)), ((), ())), preferred_element_type=jnp.float32
    )
    feature_grad = lax.psum_scatter(
        terms.astype(jnp.bfloat16), "dep", scatter_dimension=1, tiled=True
    )
    return (activations, feature_grad, weight_grad)


def solution(mesh):
    return jax.shard_map(
        per_device,
        mesh=mesh,
        in_specs=(
            P(("col", "row"), None),
            P(None, "dep"),
            P("row", "col", None, None, None),
            P("row", "col", None, None),
            P("row", "col"),
            P(("row", "col"), "dep"),
        ),
        out_specs=(P(("row", "col"), "dep"), P(("col", "row"), "dep"), P(None, "dep")),
        check_vma=False,
    )
```

profile of v0, /device:TPU:1, one launch (start us, length us, event | category | flops | bytes accessed | tf_op | source)
XLA Modules:
  0.0 707.2 jit_solution(8242887909257662587)
XLA Ops:
  7.2 0.0 copy-start
  7.2 0.0 reduce-scatter.6.cloned.1.call-start
  7.2 0.8 slice_bitcast_fusion
  8.0 0.8 fusion.26
  9.4 0.0 copy-done
  9.4 1.0 convolution_convert_fusion.1
  10.4 20.0 %all_gather.6 = bf16[2048,128]{1,0:T(8,128)(2,1)S(1)} all-gather(bf16[128,128]{1,0:T(8,128)(2,1)S(1)} %convolution_convert_fusion.1), channel_id=1, replica_groups=mesh['row'=16,'col'=16,'dep'=2] {'row'}, dimensions={0}, use_global_device_ids=true | all-gather | bytes 557056 | tf_op jit(solution)/shard_map/all_gather | solution.py:33
  30.4 3.1 gather_fusion
  33.5 9.7 %fusion.1 = (bf16[128,128,128]{1,2,0:T(8,128)(2,1)}, bf16[128,128,128]{1,2,0:T(8,128)(2,1)}) fusion(bf16[128,128,128]{2,1,0:T(8,128)(2,1)} %gather_fusion, bf16[1,1,128,128,128]{4,3,2,1,0:T(8,128)(2,1)} %param.8), kind=kOutput, calls=%fused_computation.7 | convolution fusion | flops 545259520 | bytes 16777216 | tf_op jit(solution)/shard_map/tab,tbf->taf/dot_general | solution.py:35
  43.2 6.8 copy.25
  49.9 6.6 copy.24
  56.5 0.0 copy-start.2
  56.5 3.0 fusion.15
  59.5 0.5 copy-done.2
  60.0 0.0 copy-start.4
  60.0 0.7 convolution_add_fusion.1
  60.6 1.3 copy.26
  61.9 0.0 reduce-scatter.6.cloned.1.call-update
  61.9 0.0 reduce-scatter.8.cloned.1.call-start
  62.0 68.0 %reduce-scatter.6.cloned.1.call-done = f32[128,128]{1,0:T(8,128)} async-done(((f32[2048,128]{1,0:T(8,128)}), f32[128,128]{1,0:T(8,128)}) %reduce-scatter.6.cloned.1.call-update) | async-done | bytes 65552 | tf_op jit(solution)/shard_map/reduce_scatter | solution.py:38
  130.0 0.0 copy-done.4
  130.0 1.5 multiply_convert_fusion
  131.5 24.1 %all_gather.7 = bf16[2048,128]{1,0:T(8,128)(2,1)S(1)} all-gather(bf16[128,128]{1,0:T(8,128)(2,1)S(1)} %get-tuple-element.16), channel_id=1, replica_groups=mesh['row'=16,'col'=16,'dep'=2] {'col'}, dimensions={0}, use_global_device_ids=true | all-gather | bytes 557056 | tf_op jit(solution)/shard_map/all_gather | solution.py:42
  155.6 3.1 gather_fusion.1
  158.7 8.6 %fusion = (bf16[128,128,128]{1,2,0:T(8,128)(2,1)}, bf16[128,128,128]{1,2,0:T(8,128)(2,1)}) fusion(bf16[128,128,128]{2,1,0:T(8,128)(2,1)} %gather_fusion.1, bf16[1,1,128,128,128]{4,3,2,1,0:T(8,128)(2,1)} %param.8), kind=kOutput, calls=%fused_computation.4 | convolution fusion | flops 545259520 | bytes 16777216 | tf_op jit(solution)/shard_map/tab,taf->tbf/dot_general | solution.py:44
  167.3 6.8 copy.29
  174.0 6.6 copy.28
  180.6 0.0 copy-start.1
  180.6 3.0 fusion.12
  183.6 0.5 copy-done.1
  184.1 0.0 copy-start.3
  184.1 0.7 fusion.6
  184.7 0.9 copy.30
  185.7 0.0 reduce-scatter.8.cloned.1.call-update
  185.7 0.0 all-reduce.2.cloned.1.call-start
  185.7 101.1 %reduce-scatter.8.cloned.1.call-done = bf16[128,128]{1,0:T(8,128)(2,1)} async-done(((bf16[2048,128]{1,0:T(8,128)(2,1)}), bf16[128,128]{1,0:T(8,128)(2,1)}) %reduce-scatter.8.cloned.1.call-update) | async-done | bytes 32784 | tf_op jit(solution)/shard_map/reduce_scatter | solution.py:51
  286.8 1.6 convolution_bitcast_fusion
  288.4 0.0 all-reduce.2.cloned.1.call-update
  288.5 0.0 reduce-scatter.10.cloned.1.call-start
  288.5 0.0 copy-done.3
  288.5 0.9 convolution_convert_fusion
  289.5 0.7 copy.34
  290.2 0.0 reduce-scatter.10.cloned.1.call-update
  290.2 381.4 %all-reduce.2.cloned.1.call-done = f32[256,128]{0,1:T(8,128)} async-done(((f32[256,128]{0,1:T(8,128)}), f32[256,128]{0,1:T(8,128)}) %all-reduce.2.cloned.1.call-update) | async-done | bytes 131088 | tf_op jit(solution)/shard_map/psum | solution.py:57
  671.6 1.7 copy.31
  673.2 25.9 %reduce-scatter.10.cloned.1.call-done = bf16[128,128]{1,0:T(8,128)(2,1)} async-done(((bf16[256,128]{1,0:T(8,128)(2,1)}), bf16[128,128]{1,0:T(8,128)(2,1)}) %reduce-scatter.10.cloned.1.call-update) | async-done | bytes 32784
  699.2 1.5 copy.35
  (3 shorter events, 0.0 us)
Async XLA Ops:
  7.2 2.3 copy-start
  7.2 122.9 %reduce-scatter.6.cloned.1.call-start = ((), (), s32[]{:S(2)}) async-start(), calls=%async_computation.3 | async-start | bytes 1114112 | tf_op jit(solution)/shard_map/reduce_scatter | solution.py:38
  56.5 3.4 copy-start.2
  60.0 70.1 %copy-start.4 = (bf16[128,128]{1,0:T(8,128)(2,1)S(1)}, bf16[128,128]{1,0:T(8,128)(2,1)}, u32[]{:S(2)}) copy-start(bf16[128,128]{1,0:T(8,128)(2,1)} %param.11) | copy-start | bytes 98308
  61.9 224.9 %reduce-scatter.8.cloned.1.call-start = ((), (), s32[]{:S(2)}) async-start(), calls=%async_computation.4 | async-start | bytes 557056 | tf_op jit(solution)/shard_map/reduce_scatter | solution.py:51
  180.6 3.4 copy-start.1
  184.1 104.4 %copy-start.3 = (bf16[256,128]{1,0:T(8,128)(2,1)S(1)}, bf16[256,128]{1,0:T(8,128)(2,1)}, u32[]{:S(2)}) copy-start(bf16[256,128]{1,0:T(8,128)(2,1)} %param.7) | copy-start | bytes 196612
  185.7 485.9 %all-reduce.2.cloned.1.call-start = ((), (), s32[]{:S(2)}) async-start(), calls=%async_computation.5 | async-start | bytes 262144 | tf_op jit(solution)/shard_map/psum | solution.py:57
  288.5 410.7 %reduce-scatter.10.cloned.1.call-start = ((), (), s32[]{:S(2)}) async-start(), calls=%async_computation.6 | async-start | bytes 98304
Sparse Core Ops, SparseCore 0:
  62.1 67.9 reduce-scatter.5
  185.8 100.9 reduce-scatter.7
  292.8 378.7 all-reduce.1
  674.4 24.7 reduce-scatter.9
where the time goes:
time: 708 us; the launch traced here: 707 us
  waiting for transfers between devices  576 us (81%)
  blocking collectives  44.1 us (6%)
  local copies, waits for them, and re-layouts  40.6 us (6%)
  matrix products  29.1 us (4%)
  between operations  14.5 us (2%)
    psum x1, waiting for transfers between devices, per_device(): weight_grad = lax.psum(weight_product_terms, ('row', 'col'))  381 us
    reduce_scatter x1, waiting for transfers between devices, per_device(): lax.psum_scatter(backward_partial_sum.astype(jnp.bfloat16), 'row', scatte...  101 us
    reduce_scatter x1, waiting for transfers between devices, per_device(): lax.psum_scatter(partial_value, 'col', scatter_dimension=0, tiled=True)  68 us
    unnamed x5, waiting for transfers between devices  26 us
    all_gather x1, blocking collectives, per_device(): slope_all = lax.all_gather(slope, 'col', axis=0, tiled=True)  24.1 us
    all_gather x1, blocking collectives, per_device(): source_all = lax.all_gather(projected, 'row', axis=0, tiled=True)  20 us
  transfers between devices with their start and end apart: 4, of which 4 were waited for; matrix products, arithmetic and copies ran while one was open for 0% of the time, Pallas kernels for 0%

commit v1 on v0

v1 whole, which is shorter than its diff:
```python
import functools

import jax
import jax.numpy as jnp
from jax import lax
from jax.experimental import pallas as pl
from jax.experimental.pallas import tpu as pltpu
from jax.sharding import PartitionSpec as P

MESH = pl.DeviceIdType.MESH
F32, BF16 = jnp.float32, jnp.bfloat16
B = 128
BPP = 16
NODES = BPP * B
HB = B // 2
NX, NY, NZ = 4, 4, 16
XY = sorted(
    [(dx, dy) for dx in (0, 1, -1, 2) for dy in (0, 1, -1, 2) if (dx, dy) != (0, 0)],
    key=lambda o: -(abs(o[0]) + abs(o[1])),
)
FIRST = (6, -6, 3, -3, 1, -1)
CHILDREN = {6: (8, 7, 5), -6: (-7, -5), 3: (4, 2), -3: (-4, -2), 1: (), -1: ()}
LEAVES = (8, 7, -7, 5, -5, 4, -4, 2, -2)
PARENT = {d: p for p, ds in CHILDREN.items() for d in ds}
PEERS = (
    [(dx, dy, 0, 0) for dx, dy in XY]
    + [(0, 0, d, 0) for d in range(1, NZ)]
    + [(0, 0, d, 1) for d in FIRST]
    + [(0, 0, 0, 1)]
)
N_SEMS = 15 + 9 + 13 + 3 + 13 + 9 + 15 + 1 + 15 + 15 + 15


def kernel(
    feat, weight, cot, blocks, counts, tiles, act_out, fg_out, wg_out,
    tile_v, dense, gath, inv_v, inv_s, w_all, cot_h, leaf_s, leaf_r, part, first_s, first_r, sib_s, sib_r, agg,
    act_s, act_r, slope_s, slope_p, spread_t, back_s, back_r, wgp, wg_s, wg_r, wg_t, wc_s, wc_r, wz, wt,
    tile_sem, inv_sem, send_sem, recv_sem,
):
    i = lax.axis_index("row")
    z = lax.axis_index("col")
    c = lax.axis_index("dep")
    x, y = lax.rem(i, NX), lax.div(i, NX)

    def row_at(dx, dy):
        return lax.rem(y + (dy + NY), NY) * NX + lax.rem(x + (dx + NX), NX)

    def z_at(d):
        return lax.rem(z + (d + NZ), NZ)

    def device(dx, dy, dz, dc):
        return (row_at(dx, dy), z_at(dz), 1 - c if dc else c)

    def block(at, size=B):
        return pl.ds(pl.multiple_of(at * size, size), size)

    counter = [0]
    sent = []

    def send(src, dst, where):
        k = counter[0]
        counter[0] += 1
        copy = pltpu.make_async_remote_copy(
            src_ref=src, dst_ref=dst, send_sem=send_sem.at[k], recv_sem=recv_sem.at[k],
            device_id=where, device_id_type=MESH,
        )
        copy.start()
        sent.append(copy)
        return copy

    def send_both(srcs, dst, landed, z_to):
        k = counter[0]
        counter[0] += 2
        copies = [
            pltpu.make_async_remote_copy(
                src_ref=srcs[q], dst_ref=dst, send_sem=send_sem.at[k + q], recv_sem=recv_sem.at[k + c],
                device_id=(i, z_to, jnp.int32(q)), device_id_type=MESH,
            )
            for q in range(2)
        ]
        for copy in copies:
            copy.start()
        sent.extend(copies)
        return [
            pltpu.make_async_remote_copy(
                src_ref=srcs[q], dst_ref=landed(q), send_sem=send_sem.at[k + q], recv_sem=recv_sem.at[k + q],
                device_id=(i, z_to, jnp.int32(q)), device_id_type=MESH,
            )
            for q in range(2)
        ]

    loads = []
    for q in range(4):
        load = pltpu.make_async_copy(
            tiles.at[0, 0, pl.ds(q * 32, 32)], tile_v.at[pl.ds(q * 32, 32)], tile_sem.at[q]
        )
        load.start()
        loads.append(load)
    barrier = pltpu.get_barrier_semaphore()
    for peer in PEERS:
        pl.semaphore_signal(barrier, inc=1, device_id=device(*peer), device_id_type=MESH)

    flat = blocks[0, 0, 0:1, :] * BPP + blocks[0, 0, 1:2, :]
    lane = lax.broadcasted_iota(jnp.int32, (1, B), 1)
    flat = jnp.where(lane < counts[0, 0], flat, -1)
    flat = jnp.broadcast_to(flat, (B, B)).T
    slot = lax.broadcasted_iota(jnp.int32, (B, B), 0) - B
    place = lax.broadcasted_iota(jnp.int32, (B, B), 1)
    inv_v[...] = jnp.zeros_like(inv_v)
    for h in range(2):
        hit = jnp.where(flat == place + h * B, slot, 0)
        inv_v[h : h + 1, :] = jnp.clip(jnp.sum(hit, axis=0, keepdims=True) + B, 0, B)
    inv_copy = pltpu.make_async_copy(inv_v, inv_s, inv_sem)
    inv_copy.start()
    tile_v[B] = jnp.zeros((B, B), BF16)

    own = block(i)
    gath[own, :] = feat[:, block(c)]
    w_all[c] = weight[...]
    cot_h[c] = cot[block(c, HB), :]

    pl.semaphore_wait(barrier, len(PEERS))

    gathered = [send(gath.at[own], gath.at[own], device(dx, dy, 0, 0)) for dx, dy in XY]
    got_w = send(weight, w_all.at[c], device(0, 0, 0, 1))
    got_cot = send(cot.at[block(1 - c, HB)], cot_h.at[c], device(0, 0, 0, 1))

    inv_copy.wait()
    for load in loads:
        load.wait()

    @pl.loop(0, BPP)
    def _(r):
        rows = block(r)
        for col in range(BPP):
            at = r * BPP + col
            dense[rows, col * B : (col + 1) * B] = tile_v[inv_s[lax.div(at, B), lax.rem(at, B)]]

    for copy in gathered:
        copy.wait_recv()

    def chunk(d):
        return jnp.dot(dense[block(z_at(-d)), :], gath[...], preferred_element_type=F32)

    leaf_copy = {}
    for k, d in enumerate(LEAVES):
        leaf_s[k] = chunk(d).astype(BF16)
        leaf_copy[d] = send(leaf_s.at[k], leaf_r.at[k], device(0, 0, PARENT[d] - d, 0))

    def send_first(k, p, value):
        first_s[k] = value.astype(BF16)
        halves = [first_s.at[k, pl.ds(q * HB, HB)] for q in range(2)]
        return send_both(halves, first_r.at[k, c], lambda q: first_r.at[k, q], z_at(-p))

    first_copy = {}
    for k, p in enumerate(FIRST):
        if CHILDREN[p]:
            part[k] = chunk(p)
    for k, p in enumerate(FIRST):
        if not CHILDREN[p]:
            first_copy[p] = send_first(k, p, chunk(p))
    mine = chunk(0)
    part[len(FIRST)] = mine
    sib_s[...] = part[len(FIRST), block(1 - c, HB), :].astype(BF16)
    sib_copy = send(sib_s, sib_r, device(0, 0, 0, 1))
    for p in (3, -3, 6, -6):
        k = FIRST.index(p)
        total = part[k]
        for d in CHILDREN[p]:
            leaf_copy[d].wait_recv()
            total = total + leaf_r[LEAVES.index(d)].astype(F32)
        first_copy[p] = send_first(k, p, total)
    agg[c] = part[len(FIRST), block(c, HB), :]
    sib_copy.wait_recv()
    agg[1 - c] = sib_r[...].astype(F32)
    got_w.wait_recv()
    got_cot.wait_recv()
    for p in (1, -1, 3, -3, 6, -6):
        for copy in first_copy[p]:
            copy.wait_recv()
    halves = []
    for h in range(2):
        total = agg[h]
        for k in range(len(FIRST)):
            total = total + first_r[k, h].astype(F32)
        halves.append(total.astype(BF16))

    slopes = []
    for u in range(2):
        pre = sum(
            jnp.dot(halves[h], w_all[u, h * B : (h + 1) * B, :], preferred_element_type=F32) for h in range(2)
        )
        squash = jnp.tanh(pre)
        act_s[u] = squash.astype(BF16)
        slopes.append((cot_h[u].astype(F32) * (1.0 - squash * squash)).astype(BF16))
    for h in range(2):
        back = sum(
            lax.dot_general(
                slopes[u], w_all[u, h * B : (h + 1) * B, :], (((1,), (1,)), ((), ())), preferred_element_type=F32
            )
            for u in range(2)
        )
        slope_s[h] = back.astype(BF16)

    here = pl.ds(pl.multiple_of(z * B + c * HB, HB), HB)
    out_copy = {}
    for p in FIRST:

        def landed(q, p=p):
            return slope_p.at[pl.ds(pl.multiple_of(z_at(-p) * B + q * HB, HB), HB)]

        out_copy[p] = send_both([slope_s.at[q] for q in range(2)], slope_p.at[here], landed, z_at(p))
    near = send(slope_s.at[1 - c], slope_p.at[here], device(0, 0, 0, 1))
    slope_p[here, :] = slope_s[c]
    act_copy = send(act_s.at[1 - c], act_r, device(0, 0, 0, 1))
    act_out[block(c, HB), :] = act_s[c]

    for u in range(2):
        for h in range(2):
            wgp[u, h * B : (h + 1) * B, :] = lax.dot_general(
                halves[h], slopes[u], (((0,), (0,)), ((), ())), preferred_element_type=F32
            )
    wg_s[...] = wgp[1 - c].astype(BF16)
    wg_copy = send(wg_s, wg_r, device(0, 0, 0, 1))

    leaf_out = {}
    for p in (3, -3, 6, -6):
        for copy in out_copy[p]:
            copy.wait_recv()
        rows = block(z_at(-p))
        for d in CHILDREN[p]:
            leaf_out[d] = send(slope_p.at[rows], slope_p.at[rows], device(0, 0, d - p, 0))

    wg_copy.wait_recv()
    wg_t[...] = wgp[c] + wg_r[...].astype(F32)
    wc_s[...] = wg_t[...].astype(BF16)
    wc_copy = [
        send(wc_s.at[block(row_at(dx, dy), 16)], wc_r.at[k], device(dx, dy, 0, 0))
        for k, (dx, dy) in enumerate(XY)
    ]

    near.wait_recv()
    for p in (1, -1):
        for copy in out_copy[p]:
            copy.wait_recv()
    act_copy.wait_recv()
    act_out[block(1 - c, HB), :] = act_r[...]
    for copy in wc_copy:
        copy.wait_recv()
    total = wg_t[block(i, 16), :]
    for k in range(len(XY)):
        total = total + wc_r[k].astype(F32)
    wz[z] = total.astype(BF16)
    wz_copy = [send(wz.at[z], wz.at[z], device(0, 0, d, 0)) for d in range(1, NZ)]

    for d in LEAVES:
        leaf_out[d].wait_recv()

    @pl.loop(0, 4)
    def _(q):
        cols = block(q, 512)
        value = lax.dot_general(
            slope_p[...], dense[:, cols], (((0,), (0,)), ((), ())), preferred_element_type=F32
        )
        for k in range(4):
            spread_t[q * 4 + k] = value[:, k * B : (k + 1) * B]
            back_s[q * 4 + k] = value[:, k * B : (k + 1) * B].astype(BF16)

    back_copy = [
        send(back_s.at[row_at(dx, dy)], back_r.at[k], device(dx, dy, 0, 0)) for k, (dx, dy) in enumerate(XY)
    ]

    for copy in wz_copy:
        copy.wait_recv()
    total = wz[0].astype(F32)
    for k in range(1, NZ):
        total = total + wz[k].astype(F32)
    wt[block(i, 16), :] = total
    wt_copy = [
        send(wt.at[block(i, 16)], wt.at[block(i, 16)], device(dx, dy, 0, 0)) for dx, dy in XY
    ]

    for copy in back_copy:
        copy.wait_recv()
    total = spread_t[i]
    for k in range(len(XY)):
        total = total + back_r[k].astype(F32)
    fg_out[...] = total.T.astype(BF16)

    for copy in wt_copy:
        copy.wait_recv()
    wg_out[...] = wt[...]
    for copy in sent:
        copy.wait_send()


def per_device(features, weight, tiles, tile_blocks, tile_counts, cotangent):
    vmem = pl.BlockSpec(memory_space=pltpu.VMEM)
    smem = pl.BlockSpec(memory_space=pltpu.SMEM)
    n_xy = len(XY)
    scratch = [
        pltpu.VMEM((B + 1, B, B), BF16),
        pltpu.VMEM((NODES, NODES), BF16),
        pltpu.VMEM((NODES, B), BF16),
        pltpu.VMEM((8, B), jnp.int32),
        pltpu.SMEM((8, B), jnp.int32),
        pltpu.VMEM((2, 2 * B, B), BF16),
        pltpu.VMEM((2, HB, B), BF16),
        pltpu.VMEM((9, B, B), BF16),
        pltpu.VMEM((9, B, B), BF16),
        pltpu.VMEM((7, B, B), F32),
        pltpu.VMEM((6, B, B), BF16),
        pltpu.VMEM((6, 2, HB, B), BF16),
        pltpu.VMEM((HB, B), BF16),
        pltpu.VMEM((HB, B), BF16),
        pltpu.VMEM((2, HB, B), F32),
        pltpu.VMEM((2, HB, B), BF16),
        pltpu.VMEM((HB, B), BF16),
        pltpu.VMEM((2, HB, B), BF16),
        pltpu.VMEM((NODES, B), BF16),
        pltpu.VMEM((BPP, B, B), F32),
        pltpu.VMEM((BPP, B, B), BF16),
        pltpu.VMEM((n_xy, B, B), BF16),
        pltpu.VMEM((2, 2 * B, B), F32),
        pltpu.VMEM((2 * B, B), BF16),
        pltpu.VMEM((2 * B, B), BF16),
        pltpu.VMEM((2 * B, B), F32),
        pltpu.VMEM((2 * B, B), BF16),
        pltpu.VMEM((n_xy, 16, B), BF16),
        pltpu.VMEM((NZ, 16, B), BF16),
        pltpu.VMEM((2 * B, B), F32),
        pltpu.SemaphoreType.DMA((4,)),
        pltpu.SemaphoreType.DMA,
        pltpu.SemaphoreType.DMA((N_SEMS,)),
        pltpu.SemaphoreType.DMA((N_SEMS,)),
    ]
    return tuple(
        pl.pallas_call(
            kernel,
            out_shape=(
                jax.ShapeDtypeStruct((B, B), BF16),
                jax.ShapeDtypeStruct((B, B), BF16),
                jax.ShapeDtypeStruct((2 * B, B), F32),
            ),
            in_specs=[vmem, vmem, vmem, vmem, smem, pl.BlockSpec(memory_space=pl.ANY)],
            out_specs=(vmem, vmem, vmem),
            scratch_shapes=scratch,
            compiler_params=pltpu.CompilerParams(
                collective_id=0, has_side_effects=True, vmem_limit_bytes=56 * 2**20
            ),
            cost_estimate=pl.CostEstimate(flops=4 * NODES * NODES * B, bytes_accessed=2**23, transcendentals=B * B),
            name="gcn",
        )(features, weight, cotangent, tile_blocks, tile_counts, tiles)
    )


def solution(mesh):
    return jax.shard_map(
        per_device,
        mesh=mesh,
        in_specs=(
            P(("col", "row"), None),
            P(None, "dep"),
            P("row", "col", None, None, None),
            P("row", "col", None, None),
            P("row", "col"),
            P(("row", "col"), "dep"),
        ),
        out_specs=(P(("row", "col"), "dep"), P(("col", "row"), "dep"), P(None, "dep")),
        check_vma=False,
    )
```

time: 708 us -> 78 us (0.11)
  waiting for transfers between devices: 576 us -> 0 us
  Pallas kernels: 0 us -> 72 us
  blocking collectives: 44.1 us -> 0 us
  local copies, waits for them, and re-layouts: 40.6 us -> 4.32 us
  matrix products: 29.1 us -> 0 us
  between operations: 14.5 us -> 1.29 us
    psum x1 -> x0, waiting for transfers between devices: 381 us -> none  [per_device(): weight_grad = lax.psum(weight_product_terms, ('row', 'col'))]
    reduce_scatter x2 -> x0, waiting for transfers between devices: 169 us -> none  [the longest x1 101 us: per_device(): lax.psum_scatter(backward_partial_sum.astype(jnp.bfloat16), 'row', scatte...]
    pallas_call x0 -> x1, Pallas kernels: none -> 72 us  [per_device(): pl.pallas_call(kernel, out_shape=(jax.ShapeDtypeStruct((B, B), BF16), jax...]
    all_gather x2 -> x0, blocking collectives: 44.1 us -> none  [the longest x1 24.1 us: per_device(): slope_all = lax.all_gather(slope, 'col', axis=0, tiled=True)]
    dot_general x9 -> x0, matrix products: 29.1 us -> none  [the longest x1 9.7 us: per_device(): jnp.einsum('tab,tbf->taf', tile_set, source_tiles, preferred_element_type...]
    convert_element_type x5 -> x0, local copies, waits for them, and re-layouts: 27.6 us -> none  [the longest x2 13.5 us: chosen_column_sum(): lower = (product - upper.astype(jnp.float32)).astype(jnp.bfloat16)]
    unnamed x5 -> x0, waiting for transfers between devices: 26 us -> none
  transfers between devices with their start and end apart: 4 -> 0, of which waited for: 4 -> 0; matrix products, arithmetic and copies ran while one was open for 0% -> 0% of each run, Pallas kernels for 0% -> 0%
where the time goes in v1:
time: 78 us; the launch traced here: 77.6 us
  Pallas kernels  72 us (92%)
  local copies, waits for them, and re-layouts  4.32 us (6%)
  between operations  1.29 us (2%)
    pallas_call x1, Pallas kernels, per_device(): pl.pallas_call(kernel, out_shape=(jax.ShapeDtypeStruct((B, B), BF16), jax...  72 us
    unnamed x3, local copies, waits for them, and re-layouts  4.32 us

profile of v1, /device:TPU:1, one launch (start us, length us, event | category | flops | bytes accessed | tf_op | source)
XLA Modules:
  0.0 77.6 jit_solution(9514571999543600453)
XLA Ops:
  1.3 72.0 %gcn.1 = (bf16[128,128]{1,0:T(8,128)(2,1)}, bf16[128,128]{1,0:T(8,128)(2,1)}, f32[256,128]{1,0:T(8,128)}) custom-call(bf16[128,256]{1,0:T(8,128)(2,1)} %feat.1, bf16[256,128]{1,0:T(8,128)(2,1)} %weight.1, bf16[128,128]{1,0:T(8,128)(2,1)} %cot.1, s32[1,1,2,128]{3,2,1,0:T(2,128)} %blocks.1, s32[1,1]{1,0:T(1,128)S(6)} %copy.12.counts, ...), custom_call_target="tpu_custom_call" | custom-call | flops 2147483648 | bytes 8388608 | tf_op jit(solution)/shard_map/gcn/pallas_call | solution.py:338
  73.3 1.4 %copy.13 = bf16[128,128]{1,0:T(8,128)(2,1)} copy(bf16[128,128]{1,0:T(8,128)(2,1)} %get-tuple-element.6) | data formatting | bytes 65536
  74.7 1.4 %copy.14 = bf16[128,128]{1,0:T(8,128)(2,1)} copy(bf16[128,128]{1,0:T(8,128)(2,1)} %get-tuple-element.7) | data formatting | bytes 65536
  76.1 1.6 %copy.15 = f32[256,128]{1,0:T(8,128)} copy(f32[256,128]{1,0:T(8,128)} %get-tuple-element.8) | data formatting | bytes 262144

commit v2 on v1

v2 whole, which is shorter than its diff:
```python
import functools

import jax
import jax.numpy as jnp
from jax import lax
from jax.experimental import pallas as pl
from jax.experimental.pallas import tpu as pltpu
from jax.sharding import PartitionSpec as P

MESH = pl.DeviceIdType.MESH
F32, BF16 = jnp.float32, jnp.bfloat16
B = 128
BPP = 16
NODES = BPP * B
HB = B // 2
NX, NY, NZ = 4, 4, 16
XY = sorted(
    [(dx, dy) for dx in (0, 1, -1, 2) for dy in (0, 1, -1, 2) if (dx, dy) != (0, 0)],
    key=lambda o: -(abs(o[0]) + abs(o[1])),
)
FIRST = (5, -5, 2, -2, 1, -1)
INNER = (5, -5, 2, -2)
LEAVES = (8, 7, -7, 6, -6, 4, -4, 3, -3)
CHILDREN = {5: (7, 6, 4), -5: (-7, -6, -4), 2: (3,), -2: (-3,), 1: (), -1: ()}
PARENT = {d: p for p, ds in CHILDREN.items() for d in ds}


def children(p, h):
    pairs = [(d, d - p) for d in CHILDREN[p]]
    if p == 5 and h == 0:
        pairs = [(8, 3)] + pairs
    if p == -5 and h == 1:
        pairs = [(8, -3)] + pairs
    return pairs


def way_up(d, h):
    if d == 8:
        return -3 if h == 0 else 3
    return PARENT[d] - d


PEERS = (
    [(dx, dy, 0, 0) for dx, dy in XY]
    + [(0, 0, d, 0) for d in (5, -5, 3, -3, 2, -2, 1, -1)]
    + [(0, 0, d, 1) for d in FIRST]
    + [(0, 0, 0, 1)]
)
N_SEMS = 160


def kernel(
    feat, weight, cot, blocks, counts, tiles, act_out, fg_out, wg_out,
    tile_v, dense, gath, blk_v, inv_v, inv_s, w_all, cot_v, cot_h, leaf_s, leaf_r, part, first_s, first_r,
    sib_s, sib_r, agg, act_s, act_r, slope_s, slope_p, slope_t, spread_t, back_s, back_r, wgp, wg_s, wg_r, wg_t, wc_s,
    wc_r, wz, wt, load_sem, inv_sem, send_sem, recv_sem,
):
    i = lax.axis_index("row")
    z = lax.axis_index("col")
    c = lax.axis_index("dep")
    x, y = lax.rem(i, NX), lax.div(i, NX)

    def row_at(dx, dy):
        return lax.rem(y + (dy + NY), NY) * NX + lax.rem(x + (dx + NX), NX)

    def z_at(d):
        return lax.rem(z + (d + NZ), NZ)

    def device(dx, dy, dz, dc):
        return (row_at(dx, dy), z_at(dz), 1 - c if dc else c)

    def block(at, size=B):
        return pl.ds(pl.multiple_of(at * size, size), size)

    def piece(at, h):
        return pl.ds(pl.multiple_of(at * B + h * HB, HB), HB)

    counter = [0]
    sent = []

    def slots(n):
        counter[0] += n
        return counter[0] - n

    def remote(src, dst, where, send_k, recv_k):
        return pltpu.make_async_remote_copy(
            src_ref=src, dst_ref=dst, send_sem=send_sem.at[send_k], recv_sem=recv_sem.at[recv_k],
            device_id=where, device_id_type=MESH,
        )

    def send(src, dst, where):
        k = slots(1)
        copy = remote(src, dst, where, k, k)
        copy.start()
        sent.append(copy)
        return copy

    def send_to_core(src, dst, z_to, q, k):
        copy = remote(src, dst, (i, z_to, jnp.int32(q)), k + q, k + c)
        copy.start()
        sent.append(copy)

    def expect(dst, k):
        return remote(dst, dst, (i, z, 1 - c), k, k)

    loads = []

    def load(src, dst):
        copy = pltpu.make_async_copy(src, dst, load_sem.at[len(loads)])
        copy.start()
        loads.append(copy)
        return copy

    own = block(i)
    got_blocks = load(blocks.at[0, 0], blk_v)
    got_feat = load(feat.at[:, block(c)], gath.at[own])
    own_w = load(weight, w_all.at[c])
    own_cot = load(cot, cot_v)
    got_tiles = [load(tiles.at[0, 0, pl.ds(q * 32, 32)], tile_v.at[pl.ds(q * 32, 32)]) for q in range(4)]
    barrier = pltpu.get_barrier_semaphore()
    for peer in PEERS:
        pl.semaphore_signal(barrier, inc=1, device_id=device(*peer), device_id_type=MESH)

    got_blocks.wait()
    flat = blk_v[0:1, :] * BPP + blk_v[1:2, :]
    lane = lax.broadcasted_iota(jnp.int32, (1, B), 1)
    flat = jnp.where(lane < jnp.broadcast_to(counts[...], (1, B)), flat, -1)
    flat = jnp.broadcast_to(flat, (B, B)).T
    slot = lax.broadcasted_iota(jnp.int32, (B, B), 0) - B
    place = lax.broadcasted_iota(jnp.int32, (B, B), 1)
    inv_v[...] = jnp.zeros_like(inv_v)
    for h in range(2):
        hit = jnp.where(flat == place + h * B, slot, 0)
        inv_v[h : h + 1, :] = jnp.clip(jnp.sum(hit, axis=0, keepdims=True) + B, 0, B)
    inv_copy = pltpu.make_async_copy(inv_v, inv_s, inv_sem)
    inv_copy.start()
    tile_v[B] = jnp.zeros((B, B), BF16)
    got_feat.wait()
    own_w.wait()
    own_cot.wait()
    cot_h[c] = cot_v[block(c, HB), :]

    pl.semaphore_wait(barrier, len(PEERS))

    gathered = [send(gath.at[own], gath.at[own], device(dx, dy, 0, 0)) for dx, dy in XY]
    got_w = send(w_all.at[c], w_all.at[c], device(0, 0, 0, 1))
    got_cot = send(cot_v.at[block(1 - c, HB)], cot_h.at[c], device(0, 0, 0, 1))

    inv_copy.wait()
    for copy in got_tiles:
        copy.wait()

    @pl.loop(0, BPP)
    def _(r):
        rows = block(r)
        for col in range(BPP):
            at = r * BPP + col
            dense[rows, col * B : (col + 1) * B] = tile_v[inv_s[lax.div(at, B), lax.rem(at, B)]]

    for copy in gathered:
        copy.wait_recv()

    def chunk(d):
        return jnp.dot(dense[block(z_at(-d)), :], gath[...], preferred_element_type=F32)

    halves_of = [pl.ds(h * HB, HB) for h in range(2)]
    leaf_copy = {}

    def send_leaf(d, h):
        k = LEAVES.index(d)
        leaf_copy[d, h] = send(
            leaf_s.at[k, halves_of[h]], leaf_r.at[k, halves_of[h]], device(0, 0, way_up(d, h), 0)
        )

    for k, d in enumerate(LEAVES):
        leaf_s[k] = chunk(d).astype(BF16)
        for h in range(2):
            send_leaf(d, h)
    for k, p in enumerate(FIRST):
        value = chunk(p)
        if p in INNER:
            part[k] = value
        else:
            first_s[k] = value.astype(BF16)
    part[len(FIRST)] = chunk(0)
    first_k = {p: slots(2) for p in FIRST}

    def send_first(p, h):
        k = FIRST.index(p)
        if p in INNER:
            total = part[k, halves_of[h], :]
            for d, _ in children(p, h):
                leaf_copy[d, h].wait_recv()
                total = total + leaf_r[LEAVES.index(d), halves_of[h], :].astype(F32)
            first_s[k, halves_of[h], :] = total.astype(BF16)
        send_to_core(first_s.at[k, halves_of[h]], first_r.at[k, c], z_at(-p), h, first_k[p])

    sib_s[...] = part[len(FIRST), block(1 - c, HB), :].astype(BF16)
    sib_copy = send(sib_s, sib_r, device(0, 0, 0, 1))
    agg[c] = part[len(FIRST), block(c, HB), :]
    for h in range(2):
        for p in (1, -1) + INNER:
            send_first(p, h)
    sib_copy.wait_recv()
    agg[1 - c] = sib_r[...].astype(F32)
    got_w.wait_recv()
    got_cot.wait_recv()
    for p in (1, -1, 2, -2, 5, -5):
        for q in range(2):
            expect(first_r.at[FIRST.index(p), q], first_k[p] + q).wait_recv()
    halves = []
    for h in range(2):
        total = agg[h]
        for k in range(len(FIRST)):
            total = total + first_r[k, h].astype(F32)
        halves.append(total.astype(BF16))

    slopes = []
    for u in range(2):
        pre = sum(
            jnp.dot(halves[h], w_all[u, h * B : (h + 1) * B, :], preferred_element_type=F32) for h in range(2)
        )
        squash = jnp.tanh(pre)
        act_s[u] = squash.astype(BF16)
        slopes.append((cot_h[u].astype(F32) * (1.0 - squash * squash)).astype(BF16))
    for h in range(2):
        back = sum(
            lax.dot_general(
                slopes[u], w_all[u, h * B : (h + 1) * B, :], (((1,), (1,)), ((), ())), preferred_element_type=F32
            )
            for u in range(2)
        )
        slope_s[h] = back.astype(BF16)

    here = piece(z, c)
    out_k = {p: slots(2) for p in FIRST}
    for p in FIRST:
        for q in range(2):
            send_to_core(slope_s.at[q], slope_p.at[here], z_at(p), q, out_k[p])
    near = send(slope_s.at[1 - c], slope_p.at[here], device(0, 0, 0, 1))
    slope_p[here, :] = slope_s[c]

    for u in range(2):
        for h in range(2):
            wgp[u, h * B : (h + 1) * B, :] = lax.dot_general(
                halves[h], slopes[u], (((0,), (0,)), ((), ())), preferred_element_type=F32
            )
    wg_s[...] = wgp[1 - c].astype(BF16)
    wg_copy = send(wg_s, wg_r, device(0, 0, 0, 1))
    act_copy = send(act_s.at[1 - c], act_r, device(0, 0, 0, 1))
    act_out[block(c, HB), :] = act_s[c]

    leaf_out = {}

    def forward(p, h):
        rows = piece(z_at(-p), h)
        expect(slope_p.at[rows], out_k[p] + h).wait_recv()
        for d, way in children(p, h):
            leaf_out[d, h] = send(slope_p.at[rows], slope_p.at[rows], device(0, 0, way, 0))

    wg_copy.wait_recv()
    wg_t[...] = wgp[c] + wg_r[...].astype(F32)
    wc_s[...] = wg_t[...].astype(BF16)
    wc_copy = [
        send(wc_s.at[block(row_at(dx, dy), 16)], wc_r.at[k], device(dx, dy, 0, 0))
        for k, (dx, dy) in enumerate(XY)
    ]
    for p in (2, -2, 5, -5):
        forward(p, 0)
    for copy in wc_copy:
        copy.wait_recv()
    total = wg_t[block(i, 16), :]
    for k in range(len(XY)):
        total = total + wc_r[k].astype(F32)
    wz[z] = total.astype(BF16)
    wz_first = {p: send(wz.at[z], wz.at[z], device(0, 0, p, 0)) for p in FIRST}

    for p in (2, -2, 5, -5):
        forward(p, 1)

    act_copy.wait_recv()
    act_out[block(1 - c, HB), :] = act_r[...]

    def turn(d):
        slope_t[:, block(z_at(-d))] = slope_p[block(z_at(-d)), :].T

    near.wait_recv()
    turn(0)
    for p in (1, -1):
        for q in range(2):
            expect(slope_p.at[piece(z_at(-p), q)], out_k[p] + q).wait_recv()
        turn(p)
    for p in INNER:
        turn(p)
    wz_leaf = {}
    for p in FIRST:
        wz_first[p].wait_recv()
        at = z_at(-p)
        for d, way in children(p, 0):
            wz_leaf[d] = send(wz.at[at], wz.at[at], device(0, 0, way, 0))
    for d in LEAVES[::-1]:
        for h in range(2):
            leaf_out[d, h].wait_recv()
        turn(d)

    back_copy = []
    for dy in (2, 1, -1, 0):
        group = lax.rem(y + (dy + NY), NY)
        value = jnp.dot(slope_t[...], dense[:, block(group, NX * B)], preferred_element_type=F32)
        for k in range(NX):
            back_s[group * NX + k] = value[:, k * B : (k + 1) * B].astype(BF16)
            if dy == 0:
                spread_t[k] = value[:, k * B : (k + 1) * B]
        for dx in (2, 1, -1, 0):
            if (dx, dy) != (0, 0):
                k = XY.index((dx, dy))
                back_copy.append(send(back_s.at[row_at(dx, dy)], back_r.at[k], device(dx, dy, 0, 0)))

    for d in LEAVES:
        wz_leaf[d].wait_recv()
    total = wz[0].astype(F32)
    for k in range(1, NZ):
        total = total + wz[k].astype(F32)
    wt[block(i, 16), :] = total
    wt_copy = [
        send(wt.at[block(i, 16)], wt.at[block(i, 16)], device(dx, dy, 0, 0)) for dx, dy in XY
    ]

    for copy in back_copy:
        copy.wait_recv()
    total = spread_t[x]
    for k in range(len(XY)):
        total = total + back_r[k].astype(F32)
    fg_out[...] = total.T.astype(BF16)

    for copy in wt_copy:
        copy.wait_recv()
    wg_out[...] = wt[...]
    for copy in sent:
        copy.wait_send()


def hand_on(*refs):
    n = len(refs) // 2
    for k in range(n):
        refs[n + k][...] = refs[k][...]


def per_device(features, weight, tiles, tile_blocks, tile_counts, cotangent):
    vmem = pl.BlockSpec(memory_space=pltpu.VMEM)
    hbm = pl.BlockSpec(memory_space=pl.ANY)
    n_xy = len(XY)
    scratch = [
        pltpu.VMEM((B + 1, B, B), BF16),
        pltpu.VMEM((NODES, NODES), BF16),
        pltpu.VMEM((NODES, B), BF16),
        pltpu.VMEM((2, B), jnp.int32),
        pltpu.VMEM((8, B), jnp.int32),
        pltpu.SMEM((8, B), jnp.int32),
        pltpu.VMEM((2, 2 * B, B), BF16),
        pltpu.VMEM((B, B), BF16),
        pltpu.VMEM((2, HB, B), BF16),
        pltpu.VMEM((9, B, B), BF16),
        pltpu.VMEM((9, B, B), BF16),
        pltpu.VMEM((7, B, B), F32),
        pltpu.VMEM((6, B, B), BF16),
        pltpu.VMEM((6, 2, HB, B), BF16),
        pltpu.VMEM((HB, B), BF16),
        pltpu.VMEM((HB, B), BF16),
        pltpu.VMEM((2, HB, B), F32),
        pltpu.VMEM((2, HB, B), BF16),
        pltpu.VMEM((HB, B), BF16),
        pltpu.VMEM((2, HB, B), BF16),
        pltpu.VMEM((NODES, B), BF16),
        pltpu.VMEM((B, NODES), BF16),
        pltpu.VMEM((NX, B, B), F32),
        pltpu.VMEM((BPP, B, B), BF16),
        pltpu.VMEM((n_xy, B, B), BF16),
        pltpu.VMEM((2, 2 * B, B), F32),
        pltpu.VMEM((2 * B, B), BF16),
        pltpu.VMEM((2 * B, B), BF16),
        pltpu.VMEM((2 * B, B), F32),
        pltpu.VMEM((2 * B, B), BF16),
        pltpu.VMEM((n_xy, 16, B), BF16),
        pltpu.VMEM((NZ, 16, B), BF16),
        pltpu.VMEM((2 * B, B), F32),
        pltpu.SemaphoreType.DMA((8,)),
        pltpu.SemaphoreType.DMA,
        pltpu.SemaphoreType.DMA((N_SEMS,)),
        pltpu.SemaphoreType.DMA((N_SEMS,)),
    ]
    out_shape = (
        jax.ShapeDtypeStruct((B, B), BF16),
        jax.ShapeDtypeStruct((B, B), BF16),
        jax.ShapeDtypeStruct((2 * B, B), F32),
    )
    results = pl.pallas_call(
        kernel,
        out_shape=out_shape,
        in_specs=[hbm, hbm, hbm, hbm, vmem, hbm],
        out_specs=(vmem, vmem, vmem),
        scratch_shapes=scratch,
        compiler_params=pltpu.CompilerParams(collective_id=0, has_side_effects=True, vmem_limit_bytes=56 * 2**20),
        cost_estimate=pl.CostEstimate(flops=4 * NODES * NODES * B, bytes_accessed=2**23, transcendentals=B * B),
        name="gcn",
    )(features, weight, cotangent, tile_blocks, tile_counts, tiles)
    results = pl.pallas_call(
        hand_on,
        out_shape=out_shape,
        in_specs=[vmem] * 3,
        out_specs=(vmem, vmem, vmem),
        cost_estimate=pl.CostEstimate(flops=0, bytes_accessed=2**19, transcendentals=0),
        name="hand_on",
    )(*results)
    return tuple(results)


def solution(mesh):
    return jax.shard_map(
        per_device,
        mesh=mesh,
        in_specs=(
            P(("col", "row"), None),
            P(None, "dep"),
            P("row", "col", None, None, None),
            P("row", "col", None, None),
            P("row", "col"),
            P(("row", "col"), "dep"),
        ),
        out_specs=(P(("row", "col"), "dep"), P(("col", "row"), "dep"), P(None, "dep")),
        check_vma=False,
    )
```

time: 78 us -> 69.7 us (0.89)
  local copies, waits for them, and re-layouts: 4.32 us -> 0 us
  Pallas kernels: 72 us -> 68.3 us
    unnamed x3 -> x0, local copies, waits for them, and re-layouts: 4.32 us -> none
    pallas_call x1 -> x2, Pallas kernels: 72 us -> 68.3 us  [the longest x1 66.6 us: per_device(): pl.pallas_call(kernel, out_shape=out_shape, in_specs=[hbm, hbm, hbm, hbm,...]
where the time goes in v2:
time: 69.7 us; the launch traced here: 69.5 us
  Pallas kernels  68.3 us (98%)
  between operations  1.29 us (2%)
    pallas_call x1, Pallas kernels, per_device(): pl.pallas_call(kernel, out_shape=out_shape, in_specs=[hbm, hbm, hbm, hbm,...  66.6 us
    pallas_call x1, Pallas kernels, per_device(): pl.pallas_call(hand_on, out_shape=out_shape, in_specs=[vmem] * 3, out_spe...  1.63 us

profile of v2, /device:TPU:1, one launch (start us, length us, event | category | flops | bytes accessed | tf_op | source)
XLA Modules:
  0.0 69.5 jit_solution(17118030640538260945)
XLA Ops:
  1.3 66.6 %gcn.1 = (bf16[128,128]{1,0:T(8,128)(2,1)}, bf16[128,128]{1,0:T(8,128)(2,1)}, f32[256,128]{1,0:T(8,128)}) custom-call(bf16[128,256]{1,0:T(8,128)(2,1)} %feat.1, bf16[256,128]{1,0:T(8,128)(2,1)} %weight.1, bf16[128,128]{1,0:T(8,128)(2,1)} %cot.1, s32[1,1,2,128]{3,2,1,0:T(2,128)} %blocks.1, s32[1,1]{1,0:T(1,128)S(6)} %copy.9.counts, ...), custom_call_target="tpu_custom_call" | custom-call | flops 2147483648 | bytes 8388608 | tf_op jit(solution)/shard_map/gcn/pallas_call | solution.py:397
  67.9 1.6 %hand_on.1 = (bf16[128,128]{1,0:T(8,128)(2,1)}, bf16[128,128]{1,0:T(8,128)(2,1)}, f32[256,128]{1,0:T(8,128)}) custom-call(bf16[128,128]{1,0:T(8,128)(2,1)} %get-tuple-element.6.refs_0_, bf16[128,128]{1,0:T(8,128)(2,1)} %get-tuple-element.7.refs_1_, f32[256,128]{1,0:T(8,128)} %get-tuple-element.8.refs_2_), custom_call_target="tpu_custom_call" | custom-call | bytes 524288 | tf_op jit(solution)/shard_map/hand_on/pallas_call | solution.py:407

commit v3 on v2

--- a/solution.py
+++ b/solution.py
@@ -94,6 +94,11 @@
         copy.start()
         sent.append(copy)
         return copy
+
+    def settle():
+        for copy in sent:
+            copy.wait_send()
+        sent.clear()
 
     def send_to_core(src, dst, z_to, q, k):
         copy = remote(src, dst, (i, z_to, jnp.int32(q)), k + q, k + c)
@@ -201,6 +206,10 @@
     for h in range(2):
         for p in (1, -1) + INNER:
             send_first(p, h)
+    early = sent[:-12]
+    for copy in early:
+        copy.wait_send()
+    del sent[:-12]
     sib_copy.wait_recv()
     agg[1 - c] = sib_r[...].astype(F32)
     got_w.wait_recv()
@@ -265,6 +274,10 @@
         send(wc_s.at[block(row_at(dx, dy), 16)], wc_r.at[k], device(dx, dy, 0, 0))
         for k, (dx, dy) in enumerate(XY)
     ]
+    early = sent[:-15]
+    for copy in early:
+        copy.wait_send()
+    del sent[:-15]
     for p in (2, -2, 5, -5):
         forward(p, 0)
     for copy in wc_copy:
@@ -298,6 +311,7 @@
         at = z_at(-p)
         for d, way in children(p, 0):
             wz_leaf[d] = send(wz.at[at], wz.at[at], device(0, 0, way, 0))
+    settle()
     for d in LEAVES[::-1]:
         for h in range(2):
             leaf_out[d, h].wait_recv()
@@ -305,6 +319,16 @@
 
     back_copy = []
     for dy in (2, 1, -1, 0):
+        if dy == 0:
+            for d in LEAVES:
+                wz_leaf[d].wait_recv()
+            grad = wz[0].astype(F32)
+            for k in range(1, NZ):
+                grad = grad + wz[k].astype(F32)
+            wt[block(i, 16), :] = grad
+            wt_copy = [
+                send(wt.at[block(i, 16)], wt.at[block(i, 16)], device(dx, dy, 0, 0)) for dx, dy in XY
+            ]
         group = lax.rem(y + (dy + NY), NY)
         value = jnp.dot(slope_t[...], dense[:, block(group, NX * B)], preferred_element_type=F32)
         for k in range(NX):
@@ -316,16 +340,6 @@
                 k = XY.index((dx, dy))
                 back_copy.append(send(back_s.at[row_at(dx, dy)], back_r.at[k], device(dx, dy, 0, 0)))
 
-    for d in LEAVES:
-        wz_leaf[d].wait_recv()
-    total = wz[0].astype(F32)
-    for k in range(1, NZ):
-        total = total + wz[k].astype(F32)
-    wt[block(i, 16), :] = total
-    wt_copy = [
-        send(wt.at[block(i, 16)], wt.at[block(i, 16)], device(dx, dy, 0, 0)) for dx, dy in XY
-    ]
-
     for copy in back_copy:
         copy.wait_recv()
     total = spread_t[x]
@@ -336,8 +350,7 @@
     for copy in wt_copy:
         copy.wait_recv()
     wg_out[...] = wt[...]
-    for copy in sent:
-        copy.wait_send()
+    settle()
 
 
 def hand_on(*refs):
@@ -396,7 +409,7 @@
     )
     results = pl.pallas_call(
         kernel,
-        out_shape=out_shape,
+        out_shape=(pltpu.VMEM((B, B), BF16), pltpu.VMEM((B, B), BF16), pltpu.VMEM((2 * B, B), F32)),
         in_specs=[hbm, hbm, hbm, hbm, vmem, hbm],
         out_specs=(vmem, vmem, vmem),
         scratch_shapes=scratch,
@@ -411,7 +424,7 @@
         out_specs=(vmem, vmem, vmem),
         cost_estimate=pl.CostEstimate(flops=0, bytes_accessed=2**19, transcendentals=0),
         name="hand_on",
-    )(*results)
+    )(*[pltpu.with_memory_space_constraint(r, pltpu.VMEM) for r in results])
     return tuple(results)
 
 

time: 69.7 us -> 67.8 us (0.973)
  Pallas kernels: 68.3 us -> 66.3 us
    pallas_call x1, Pallas kernels: 66.6 us -> 65.6 us  [per_device(): pl.pallas_call(kernel, out_shape=(pltpu.VMEM((B, B), BF16), pltpu.VMEM((B...]
    pallas_call x1, Pallas kernels: 1.63 us -> 0.69 us  [per_device(): pl.pallas_call(hand_on, out_shape=out_shape, in_specs=[vmem] * 3, out_spe...]
where the time goes in v3:
time: 67.8 us; the launch traced here: 67.6 us
  Pallas kernels  66.3 us (98%)
  between operations  1.29 us (2%)
    pallas_call x1, Pallas kernels, per_device(): pl.pallas_call(kernel, out_shape=(pltpu.VMEM((B, B), BF16), pltpu.VMEM((B...  65.6 us

profile of v3, /device:TPU:1, one launch (start us, length us, event | category | flops | bytes accessed | tf_op | source)
XLA Modules:
  0.0 67.6 jit_solution(4001991614764161413)
XLA Ops:
  1.3 65.6 %gcn.1 = (bf16[128,128]{1,0:T(8,128)(2,1)S(1)}, bf16[128,128]{1,0:T(8,128)(2,1)S(1)}, f32[256,128]{1,0:T(8,128)S(1)}) custom-call(bf16[128,256]{1,0:T(8,128)(2,1)} %feat.1, bf16[256,128]{1,0:T(8,128)(2,1)} %weight.1, bf16[128,128]{1,0:T(8,128)(2,1)} %cot.1, s32[1,1,2,128]{3,2,1,0:T(2,128)} %blocks.1, s32[1,1]{1,0:T(1,128)S(6)} %copy.9.counts, ...), custom_call_target="tpu_custom_call" | custom-call | flops 2147483648 | bytes 8388608 | tf_op jit(solution)/shard_map/gcn/pallas_call | solution.py:410
  66.9 0.7 %hand_on.1 = (bf16[128,128]{1,0:T(8,128)(2,1)}, bf16[128,128]{1,0:T(8,128)(2,1)}, f32[256,128]{1,0:T(8,128)}) custom-call(bf16[128,128]{1,0:T(8,128)(2,1)S(1)} %get-tuple-element.6.refs_0_, bf16[128,128]{1,0:T(8,128)(2,1)S(1)} %get-tuple-element.7.refs_1_, f32[256,128]{1,0:T(8,128)S(1)} %get-tuple-element.8.refs_2_), custom_call_target="tpu_custom_call" | custom-call | bytes 524288 | tf_op jit(solution)/shard_map/hand_on/pallas_call | solution.py:420

commit v4 on v3

--- a/solution.py
+++ b/solution.py
@@ -18,33 +18,37 @@
     [(dx, dy) for dx in (0, 1, -1, 2) for dy in (0, 1, -1, 2) if (dx, dy) != (0, 0)],
     key=lambda o: -(abs(o[0]) + abs(o[1])),
 )
-FIRST = (5, -5, 2, -2, 1, -1)
-INNER = (5, -5, 2, -2)
-LEAVES = (8, 7, -7, 6, -6, 4, -4, 3, -3)
-CHILDREN = {5: (7, 6, 4), -5: (-7, -6, -4), 2: (3,), -2: (-3,), 1: (), -1: ()}
+TREE = {5: (7, 6, 4), 2: (3,), 1: ()}
+FAR = max(TREE)
+CHILDREN = {s * p: tuple(s * d for d in ds) for p, ds in TREE.items() for s in (1, -1)}
+FIRST = tuple(CHILDREN)
+INNER = tuple(p for p in FIRST if CHILDREN[p] or abs(p) == FAR)
+NEAR = tuple(p for p in FIRST if p not in INNER)
 PARENT = {d: p for p, ds in CHILDREN.items() for d in ds}
+LEAVES = (8,) + tuple(sorted(PARENT, key=lambda d: (-abs(d), -d)))
 
 
 def children(p, h):
     pairs = [(d, d - p) for d in CHILDREN[p]]
-    if p == 5 and h == 0:
-        pairs = [(8, 3)] + pairs
-    if p == -5 and h == 1:
-        pairs = [(8, -3)] + pairs
+    if p == FAR and h == 0:
+        pairs = [(8, 8 - FAR)] + pairs
+    if p == -FAR and h == 1:
+        pairs = [(8, FAR - 8)] + pairs
     return pairs
 
 
 def way_up(d, h):
     if d == 8:
-        return -3 if h == 0 else 3
+        return FAR - 8 if h == 0 else 8 - FAR
     return PARENT[d] - d
 
 
-PEERS = (
+PEERS = sorted(
     [(dx, dy, 0, 0) for dx, dy in XY]
-    + [(0, 0, d, 0) for d in (5, -5, 3, -3, 2, -2, 1, -1)]
+    + [(0, 0, d, 0) for d in sorted({w for p in FIRST for h in range(2) for _, w in children(p, h)} | set(FIRST))]
     + [(0, 0, d, 1) for d in FIRST]
-    + [(0, 0, 0, 1)]
+    + [(0, 0, 0, 1)],
+    key=lambda o: -sum(map(abs, o)),
 )
 N_SEMS = 160
 
@@ -108,6 +112,9 @@
     def expect(dst, k):
         return remote(dst, dst, (i, z, 1 - c), k, k)
 
+    barrier = pltpu.get_barrier_semaphore()
+    for peer in PEERS:
+        pl.semaphore_signal(barrier, inc=1, device_id=device(*peer), device_id_type=MESH)
     loads = []
 
     def load(src, dst):
@@ -122,9 +129,6 @@
     own_w = load(weight, w_all.at[c])
     own_cot = load(cot, cot_v)
     got_tiles = [load(tiles.at[0, 0, pl.ds(q * 32, 32)], tile_v.at[pl.ds(q * 32, 32)]) for q in range(4)]
-    barrier = pltpu.get_barrier_semaphore()
-    for peer in PEERS:
-        pl.semaphore_signal(barrier, inc=1, device_id=device(*peer), device_id_type=MESH)
 
     got_blocks.wait()
     flat = blk_v[0:1, :] * BPP + blk_v[1:2, :]
@@ -204,7 +208,7 @@
     sib_copy = send(sib_s, sib_r, device(0, 0, 0, 1))
     agg[c] = part[len(FIRST), block(c, HB), :]
     for h in range(2):
-        for p in (1, -1) + INNER:
+        for p in NEAR + INNER:
             send_first(p, h)
     early = sent[:-12]
     for copy in early:
@@ -214,7 +218,7 @@
     agg[1 - c] = sib_r[...].astype(F32)
     got_w.wait_recv()
     got_cot.wait_recv()
-    for p in (1, -1, 2, -2, 5, -5):
+    for p in FIRST:
         for q in range(2):
             expect(first_r.at[FIRST.index(p), q], first_k[p] + q).wait_recv()
     halves = []
@@ -278,7 +282,7 @@
     for copy in early:
         copy.wait_send()
     del sent[:-15]
-    for p in (2, -2, 5, -5):
+    for p in INNER:
         forward(p, 0)
     for copy in wc_copy:
         copy.wait_recv()
@@ -288,7 +292,7 @@
     wz[z] = total.astype(BF16)
     wz_first = {p: send(wz.at[z], wz.at[z], device(0, 0, p, 0)) for p in FIRST}
 
-    for p in (2, -2, 5, -5):
+    for p in INNER:
         forward(p, 1)
 
     act_copy.wait_recv()
@@ -299,7 +303,7 @@
 
     near.wait_recv()
     turn(0)
-    for p in (1, -1):
+    for p in NEAR:
         for q in range(2):
             expect(slope_p.at[piece(z_at(-p), q)], out_k[p] + q).wait_recv()
         turn(p)
@@ -325,7 +329,7 @@
             grad = wz[0].astype(F32)
             for k in range(1, NZ):
                 grad = grad + wz[k].astype(F32)
-            wt[block(i, 16), :] = grad
+            wt[block(i, 16), :] = grad.astype(BF16)
             wt_copy = [
                 send(wt.at[block(i, 16)], wt.at[block(i, 16)], device(dx, dy, 0, 0)) for dx, dy in XY
             ]
@@ -349,7 +353,7 @@
 
     for copy in wt_copy:
         copy.wait_recv()
-    wg_out[...] = wt[...]
+    wg_out[...] = wt[...].astype(F32)
     settle()
 
 
@@ -373,11 +377,11 @@
         pltpu.VMEM((2, 2 * B, B), BF16),
         pltpu.VMEM((B, B), BF16),
         pltpu.VMEM((2, HB, B), BF16),
-        pltpu.VMEM((9, B, B), BF16),
-        pltpu.VMEM((9, B, B), BF16),
-        pltpu.VMEM((7, B, B), F32),
-        pltpu.VMEM((6, B, B), BF16),
-        pltpu.VMEM((6, 2, HB, B), BF16),
+        pltpu.VMEM((len(LEAVES), B, B), BF16),
+        pltpu.VMEM((len(LEAVES), B, B), BF16),
+        pltpu.VMEM((len(FIRST) + 1, B, B), F32),
+        pltpu.VMEM((len(FIRST), B, B), BF16),
+        pltpu.VMEM((len(FIRST), 2, HB, B), BF16),
         pltpu.VMEM((HB, B), BF16),
         pltpu.VMEM((HB, B), BF16),
         pltpu.VMEM((2, HB, B), F32),
@@ -396,7 +400,7 @@
         pltpu.VMEM((2 * B, B), BF16),
         pltpu.VMEM((n_xy, 16, B), BF16),
         pltpu.VMEM((NZ, 16, B), BF16),
-        pltpu.VMEM((2 * B, B), F32),
+        pltpu.VMEM((2 * B, B), BF16),
         pltpu.SemaphoreType.DMA((8,)),
         pltpu.SemaphoreType.DMA,
         pltpu.SemaphoreType.DMA((N_SEMS,)),

time: 67.8 us -> 66.9 us (0.987)
  Pallas kernels: 66.3 us -> 65.5 us
    pallas_call x1, Pallas kernels: 65.6 us -> 64.8 us  [per_device(): pl.pallas_call(kernel, out_shape=(pltpu.VMEM((B, B), BF16), pltpu.VMEM((B...]
where the time goes in v4:
time: 66.9 us; the launch traced here: 66.8 us
  Pallas kernels  65.5 us (98%)
  between operations  1.29 us (2%)
    pallas_call x1, Pallas kernels, per_device(): pl.pallas_call(kernel, out_shape=(pltpu.VMEM((B, B), BF16), pltpu.VMEM((B...  64.8 us

profile of v4, /device:TPU:1, one launch (start us, length us, event | category | flops | bytes accessed | tf_op | source)
XLA Modules:
  0.0 66.8 jit_solution(10457198860098210257)
XLA Ops:
  1.3 64.8 %gcn.1 = (bf16[128,128]{1,0:T(8,128)(2,1)S(1)}, bf16[128,128]{1,0:T(8,128)(2,1)S(1)}, f32[256,128]{1,0:T(8,128)S(1)}) custom-call(bf16[128,256]{1,0:T(8,128)(2,1)} %feat.1, bf16[256,128]{1,0:T(8,128)(2,1)} %weight.1, bf16[128,128]{1,0:T(8,128)(2,1)} %cot.1, s32[1,1,2,128]{3,2,1,0:T(2,128)} %blocks.1, s32[1,1]{1,0:T(1,128)S(6)} %copy.9.counts, ...), custom_call_target="tpu_custom_call" | custom-call | flops 2147483648 | bytes 8388608 | tf_op jit(solution)/shard_map/gcn/pallas_call | solution.py:414
  66.1 0.7 %hand_on.1 = (bf16[128,128]{1,0:T(8,128)(2,1)}, bf16[128,128]{1,0:T(8,128)(2,1)}, f32[256,128]{1,0:T(8,128)}) custom-call(bf16[128,128]{1,0:T(8,128)(2,1)S(1)} %get-tuple-element.6.refs_0_, bf16[128,128]{1,0:T(8,128)(2,1)S(1)} %get-tuple-element.7.refs_1_, f32[256,128]{1,0:T(8,128)S(1)} %get-tuple-element.8.refs_2_), custom_call_target="tpu_custom_call" | custom-call | bytes 524288 | tf_op jit(solution)/shard_map/hand_on/pallas_call | solution.py:424

commit v5 on v4

--- a/solution.py
+++ b/solution.py
@@ -16,7 +16,7 @@
 NX, NY, NZ = 4, 4, 16
 XY = sorted(
     [(dx, dy) for dx in (0, 1, -1, 2) for dy in (0, 1, -1, 2) if (dx, dy) != (0, 0)],
-    key=lambda o: -(abs(o[0]) + abs(o[1])),
+    key=lambda o: (-(abs(o[0]) + abs(o[1])), (o[0] + 2 * o[1]) % 5),
 )
 TREE = {5: (7, 6, 4), 2: (3,), 1: ()}
 FAR = max(TREE)

time: 66.9 us -> 67.7 us (1.012)
  Pallas kernels: 65.5 us -> 66.3 us
    pallas_call x1, Pallas kernels: 64.8 us -> 65.6 us  [per_device(): pl.pallas_call(kernel, out_shape=(pltpu.VMEM((B, B), BF16), pltpu.VMEM((B...]
where the time goes in v5:
time: 67.7 us; the launch traced here: 67.5 us
  Pallas kernels  66.3 us (98%)
  between operations  1.29 us (2%)
    pallas_call x1, Pallas kernels, per_device(): pl.pallas_call(kernel, out_shape=(pltpu.VMEM((B, B), BF16), pltpu.VMEM((B...  65.6 us

profile of v5, /device:TPU:1, one launch (start us, length us, event | category | flops | bytes accessed | tf_op | source)
XLA Modules:
  0.0 67.5 jit_solution(1977070317117088276)
XLA Ops:
  1.3 65.6 %gcn.1 = (bf16[128,128]{1,0:T(8,128)(2,1)S(1)}, bf16[128,128]{1,0:T(8,128)(2,1)S(1)}, f32[256,128]{1,0:T(8,128)S(1)}) custom-call(bf16[128,256]{1,0:T(8,128)(2,1)} %feat.1, bf16[256,128]{1,0:T(8,128)(2,1)} %weight.1, bf16[128,128]{1,0:T(8,128)(2,1)} %cot.1, s32[1,1,2,128]{3,2,1,0:T(2,128)} %blocks.1, s32[1,1]{1,0:T(1,128)S(6)} %copy.9.counts, ...), custom_call_target="tpu_custom_call" | custom-call | flops 2147483648 | bytes 8388608 | tf_op jit(solution)/shard_map/gcn/pallas_call | solution.py:414
  66.9 0.7 %hand_on.1 = (bf16[128,128]{1,0:T(8,128)(2,1)}, bf16[128,128]{1,0:T(8,128)(2,1)}, f32[256,128]{1,0:T(8,128)}) custom-call(bf16[128,128]{1,0:T(8,128)(2,1)S(1)} %get-tuple-element.6.refs_0_, bf16[128,128]{1,0:T(8,128)(2,1)S(1)} %get-tuple-element.7.refs_1_, f32[256,128]{1,0:T(8,128)S(1)} %get-tuple-element.8.refs_2_), custom_call_target="tpu_custom_call" | custom-call | bytes 524288 | tf_op jit(solution)/shard_map/hand_on/pallas_call | solution.py:424
